TPU v7x, 32 devices: a whole 2x2x4 slice. The times are simulated.
32 devices in a mesh: parts: 2 (over x), store: 16 (over z, y, core).
Axes of the slice: x: 2, y: 2, z: 4, core: 2. Of those that a mesh axis runs over, the one named last changes fastest.
Arguments:
- queries: bfloat16 [8, 8, 64, 128], P(None, 'parts'), parts along dimension 1, may hold values from -6 to 6
- new_keys: bfloat16 [8, 8, 8, 128], P(None, 'parts'), parts along dimension 1, may hold values from -30 to 30
- new_values: bfloat16 [8, 8, 8, 128], P(None, 'parts'), parts along dimension 1, may hold values from -6 to 6
- key_factors: bfloat16 [8, 8192, 160], P('parts', 'store'), parts along dimension 0, may hold values from -6 to 6
- key_basis: bfloat16 [8, 160, 1024], P('parts'), parts along dimension 0, may hold values from -0.5 to 0.5
- values: bfloat16 [8, 8192, 1024], P('parts', 'store'), parts along dimension 0, may hold values from -6 to 6
- block_index: int32 [8, 8, 8, 64], P(None, 'parts'), parts along dimension 1, may hold values from 0 to 1023, as said below
- block_count: int32 [8, 8, 8], P(None, 'parts'), parts along dimension 1, may hold values from 4 to 64
- out_weight: bfloat16 [8192, 8192], P('store'), may hold values from -0.75 to 0.75
Outputs:
- attn_out: bfloat16 [8, 8, 8192], P(None, 'parts', 'store'), parts along dimension 1
There are 2 independent parts, one for each index of `parts`. A program takes and returns all parts, laid end to end along the dimension named above; an argument that names none is the same for every part. Nothing has to cross between parts.
Inputs may be any that keep to these rules, and one draw needn't show every extreme that they name: `block_index`: each list holds 64 distinct block numbers; block c covers tokens 8 c to 8 c + 7. Entries at or past block_count are padding and are ignored. Among the valid entries of one list at most 4 blocks lie in the tokens of one store shard, and in every list some shard holds exactly 4 of them.
All inputs are finite; a program needn't handle non-finite values.
Results may differ from a plain program's by a relative error of at most 0.012.
The roundings to bfloat16 on the way count: a program that leaves them out, or rounds other values in their place, can miss the bound.
Values may be sent and summed in bfloat16 or wider, within the bound.
A program may use at most 128 MiB of HBM per device.

v0:
```python
import functools
import math

import jax
import jax.numpy as jnp
import numpy as np
from jax import lax
from jax.experimental import pallas as pl
from jax.experimental.pallas import tpu as pltpu
from jax.sharding import PartitionSpec as P

BLOCK = 8
ROPE_THETA = 500000.0
NEG_FLOOR = -1e30
MESH = pl.DeviceIdType.MESH


def rope_freqs(head_dim):
    exponent = np.arange(head_dim // 2, dtype=np.float64) * (2.0 / head_dim)
    base = np.power(ROPE_THETA, -exponent)
    wavelength = 2.0 * math.pi / base
    smooth = (8192.0 / wavelength - 1.0) / 3.0
    middle = (1.0 - smooth) * base / 8.0 + smooth * base
    freqs = np.where(wavelength < 2048.0, base, np.where(wavelength > 8192.0, base / 8.0, middle))
    return freqs.astype(np.float32).astype(np.float64)


def rope_tables(positions, head_dim):
    angles = positions[:, None].astype(np.float64) * rope_freqs(head_dim)[None, :]
    cosine, sine = np.cos(angles), np.sin(angles)
    return (
        np.concatenate([cosine, cosine], -1).astype(np.float32),
        np.concatenate([sine, sine], -1).astype(np.float32),
    )


def rotate(x, cosine, signed_sine):
    half = x.shape[-1] // 2
    swapped = jnp.concatenate([x[..., half:], x[..., :half]], axis=-1)
    return x * cosine + swapped * signed_sine


def attend_kernel(
    steps, head_dim, me_ref, base_ref, cos_ref, sin_ref, expand_ref, q_ref, nk_ref, nv_ref,
    mask_ref, factor_ref, basis_ref, value_ref, out_ref, stat_ref, cos_s, sin_s,
):
    r = pl.program_id(0)
    tokens = factor_ref.shape[1]
    pairs = q_ref.shape[1]
    rows = q_ref.shape[2]
    half = rows // 2
    part = half // 2
    wide = 2 * head_dim
    scale = head_dim ** -0.5
    lanes = stat_ref.shape[3]

    @pl.when(r == 0)
    def _():
        sign = jnp.where(
            lax.broadcasted_iota(jnp.int32, (tokens, head_dim), 1) < head_dim // 2, -1.0, 1.0
        )
        base_cos, base_sin = base_ref[0:1], base_ref[1:2]
        c, s = cos_ref[...], sin_ref[...]
        cos_s[...] = base_cos * c - base_sin * s
        sin_s[...] = (base_sin * c + base_cos * s) * sign
        stat_ref[...] = jnp.zeros_like(stat_ref)

    cosine, sine = cos_s[...], sin_s[...]
    holds_new = me_ref[0] == 0
    step_of = lax.broadcasted_iota(jnp.int32, (rows, steps), 0) % steps
    fresh_ok = (lax.broadcasted_iota(jnp.int32, (rows, steps), 1) <= step_of) & holds_new
    spot = lax.broadcasted_iota(jnp.int32, (part, lanes), 1) == (
        lax.broadcasted_iota(jnp.int32, (part, lanes), 0) + r * part
    )
    factors = factor_ref[0]
    for p in range(pairs):
        cols = slice(p * wide, (p + 1) * wide)
        keys = jnp.dot(factors, basis_ref[0, :, cols], preferred_element_type=jnp.float32)
        turned = []
        for u in range(2):
            k = keys[:, u * head_dim : (u + 1) * head_dim]
            turned.append(
                (k * cosine + pltpu.roll(k, head_dim // 2, 1) * sine).astype(jnp.bfloat16)
            )
        keys = jnp.concatenate(turned, axis=1)
        q = q_ref[0, p]
        zero = jnp.zeros((half, head_dim), q.dtype)
        q = jnp.concatenate(
            [jnp.concatenate([q[:half], zero], 1), jnp.concatenate([zero, q[half:]], 1)], 0
        )
        contract = (((1,), (1,)), ((), ()))
        scores = lax.dot_general(q, keys, contract, preferred_element_type=jnp.float32) * scale
        bias = jnp.dot(mask_ref[0, p], expand_ref[...], preferred_element_type=jnp.float32)
        scores = (
            scores.reshape(2, half // steps, steps, tokens) + bias.reshape(2, 1, steps, tokens)
        ).reshape(rows, tokens)
        fresh = (
            lax.dot_general(q, nk_ref[0, :, cols], contract, preferred_element_type=jnp.float32)
            * scale
        )
        fresh = jnp.where(fresh_ok, fresh, NEG_FLOOR)
        top = jnp.maximum(
            jnp.max(scores, axis=1, keepdims=True), jnp.max(fresh, axis=1, keepdims=True)
        )
        weights = jnp.exp(scores - top).astype(jnp.bfloat16)
        fresh_weights = jnp.exp(fresh - top).astype(jnp.bfloat16)
        total = jnp.sum(weights.astype(jnp.float32), axis=1, keepdims=True) + jnp.sum(
            fresh_weights.astype(jnp.float32), axis=1, keepdims=True
        )
        out = jnp.dot(weights, value_ref[0, :, cols], preferred_element_type=jnp.float32)
        out = out + jnp.dot(fresh_weights, nv_ref[0, :, cols], preferred_element_type=jnp.float32)
        for u in range(2):
            for c in range(2):
                at = u * half + c * part
                out_ref[c, 2 * p + u, 0] = out[
                    at : at + part, u * head_dim : (u + 1) * head_dim
                ].astype(out_ref.dtype)
                for i, column in enumerate((top, total)):
                    stat_ref[c, 2 * p + u, i : i + 1] += jnp.sum(
                        jnp.where(spot, column[at : at + part], 0.0), axis=0, keepdims=True
                    )


def combine_kernel(
    chips, reqs, steps, o_ref, st_ref, w_ref, out_ref, w_s, o1, st1, o2s, st2s, o2r, st2r,
    t1s, t1r, t2s, t2r, w_sem, s_o1, r_o1, s_st1, r_st1, s_o2, r_o2, s_st2, r_st2,
    s_t1, r_t1, s_t2, r_t2,
):
    me = lax.axis_index("store")
    chip, core = me // 2, me % 2
    twin = chip * 2 + 1 - core
    rows = o_ref.shape[2]
    head_dim = o_ref.shape[3]
    heads = rows // (reqs * steps)
    width = out_ref.shape[1]

    weight_copy = pltpu.make_async_copy(w_ref, w_s, w_sem)
    weight_copy.start()

    def chip_at(i):
        return lax.rem(chip + i, chips)

    def remote(src, dst, send, recv, device):
        return pltpu.make_async_remote_copy(
            src_ref=src, dst_ref=dst, send_sem=send, recv_sem=recv,
            device_id={"store": device}, device_id_type=MESH,
        )

    barrier = pltpu.get_barrier_semaphore()
    pl.semaphore_signal(barrier, inc=1, device_id={"store": twin}, device_id_type=MESH)

    def greet(i, carry):
        pl.semaphore_signal(
            barrier, inc=1, device_id={"store": chip_at(i) * 2 + core}, device_id_type=MESH
        )
        return carry

    lax.fori_loop(1, chips, greet, 0)
    pl.semaphore_wait(barrier, chips)

    def first(k):
        return (
            remote(o_ref.at[1 - core, k], o1.at[k], s_o1.at[k], r_o1.at[k], twin),
            remote(st_ref.at[1 - core, k], st1.at[k], s_st1.at[k], r_st1.at[k], twin),
        )

    def second(k, slot):
        device = k * 2 + core
        return (
            remote(o2s.at[k], o2r.at[slot], s_o2.at[k], r_o2.at[slot], device),
            remote(st2s.at[k], st2r.at[slot], s_st2.at[k], r_st2.at[slot], device),
        )

    def third(k):
        return remote(t1s.at[k], t1r.at[k], s_t1.at[k], r_t1.at[k], twin)

    def fourth(k, slot):
        return remote(t2s.at[k], t2r.at[slot], s_t2.at[k], r_t2.at[slot], k * 2 + core)

    def send_first(i, carry):
        for copy in first(chip_at(i)):
            copy.start()
        return carry

    lax.fori_loop(1, chips + 1, send_first, 0)

    def merged(k):
        for copy in first(k):
            copy.wait_recv()
        a, b = st_ref[core, k], st1[k]
        top = jnp.maximum(a[0:1], b[0:1])
        scale_a, scale_b = jnp.exp(a[0:1] - top), jnp.exp(b[0:1] - top)
        total = scale_a * a[1:2] + scale_b * b[1:2]
        pad = jnp.zeros((6, rows), jnp.float32)
        columns = jnp.concatenate([scale_a, scale_b, pad], 0).T
        mixed = (
            o_ref[core, k].astype(jnp.float32) * columns[:, 0:1]
            + o1[k].astype(jnp.float32) * columns[:, 1:2]
        )
        return mixed.astype(jnp.bfloat16), jnp.concatenate([top, total, pad], 0)

    def send_second(i, carry):
        k = chip_at(i)
        o2s[k], st2s[k] = merged(k)
        for copy in second(k, chip):
            copy.start()
        return carry

    lax.fori_loop(1, chips, send_second, 0)
    o2r[chip], st2r[chip] = merged(chip)

    def wait_second(i, carry):
        k = chip_at(i)
        for copy in second(k, k):
            copy.wait_recv()
        return carry

    lax.fori_loop(1, chips, wait_second, 0)
    tops = st2r[:, 0, :]
    share = jnp.exp(tops - jnp.max(tops, axis=0, keepdims=True))
    share = share / jnp.sum(share * st2r[:, 1, :], axis=0, keepdims=True)
    columns = share.T
    attn = o2r[0].astype(jnp.float32) * columns[:, 0:1]
    for k in range(1, chips):
        attn = attn + o2r[k].astype(jnp.float32) * columns[:, k : k + 1]
    flat = jnp.concatenate(
        [
            jnp.concatenate(
                [
                    attn[(r * heads + j) * steps : (r * heads + j + 1) * steps]
                    for r in range(reqs)
                ],
                0,
            )
            for j in range(heads)
        ],
        1,
    ).astype(jnp.bfloat16)
    weight_copy.wait()

    def term(k, which):
        at = pl.multiple_of((2 * k + which) * width, width)
        return jnp.dot(flat, w_s[:, pl.ds(at, width)], preferred_element_type=jnp.float32)

    def send_third(i, carry):
        k = chip_at(i)
        t1s[k] = term(k, 1 - core).astype(jnp.bfloat16)
        third(k).start()
        return carry

    lax.fori_loop(1, chips + 1, send_third, 0)

    def summed(k):
        mine = term(k, core)
        third(k).wait_recv()
        return mine + t1r[k].astype(jnp.float32)

    def send_fourth(i, carry):
        k = chip_at(i)
        t2s[k] = summed(k).astype(jnp.bfloat16)
        fourth(k, chip).start()
        return carry

    lax.fori_loop(1, chips, send_fourth, 0)
    own = summed(chip)

    def add_fourth(i, total):
        k = chip_at(i)
        fourth(k, k).wait_recv()
        return total + t2r[k].astype(jnp.float32)

    out_ref[...] = lax.fori_loop(1, chips, add_fourth, own).astype(out_ref.dtype)

    def drain(i, carry):
        k = chip_at(i)
        for copy in first(k) + second(k, k) + (third(k), fourth(k, k)):
            copy.wait_send()
        return carry

    lax.fori_loop(1, chips, drain, 0)
    for copy in first(chip) + (third(chip),):
        copy.wait_send()


def per_device(
    queries, new_keys, new_values, key_factors, key_basis, values, block_index, block_count,
    out_weight,
):
    devices = lax.axis_size("store")
    me = lax.axis_index("store")
    chips = devices // 2
    steps, reqs, n_heads, head_dim = queries.shape
    groups = new_keys.shape[2]
    group = n_heads // groups
    tokens = values.shape[1]
    rank = key_factors.shape[2]
    blocks = tokens // BLOCK
    heads_dev = n_heads // devices
    slots = block_index.shape[-1]
    pairs = groups // 2
    half_group = group // 2
    rows = 2 * group * steps
    part = half_group * steps
    wide = groups * head_dim
    chips_group = half_group // heads_dev

    cos_off, sin_off = rope_tables(np.arange(tokens), head_dim)
    base_tab = np.stack(rope_tables(np.arange(devices) * tokens, head_dim), 1)
    base = lax.dynamic_index_in_dim(jnp.asarray(base_tab), me, 0, keepdims=False)
    sign = np.where(np.arange(head_dim) < head_dim // 2, -1.0, 1.0).astype(np.float32)
    cos_new, sin_new = rope_tables(tokens * devices + np.arange(steps), head_dim)
    cos_new, sin_new = cos_new[:, None, None], (sin_new * sign)[:, None, None]
    q_rot = rotate(queries.astype(jnp.float32), cos_new, sin_new).astype(jnp.bfloat16)
    new_rot = rotate(new_keys.astype(jnp.float32), cos_new, sin_new).astype(jnp.bfloat16)
    q_rot = q_rot.reshape(steps, reqs, groups, chips_group, 2, heads_dev, head_dim)
    q_rot = q_rot.transpose(1, 2, 4, 3, 5, 0, 6).reshape(reqs, pairs, rows, head_dim)
    new_rot = new_rot.transpose(1, 0, 2, 3).reshape(reqs, steps, wide)
    new_val = new_values.transpose(1, 0, 2, 3).reshape(reqs, steps, wide)
    local = block_index - me * blocks
    local = jnp.where(jnp.arange(slots, dtype=jnp.int32) < block_count[..., None], local, -1)
    chosen = jnp.any(local[..., None, :] == jnp.arange(blocks, dtype=jnp.int32)[:, None], axis=-1)
    mask = jnp.where(chosen, 0.0, NEG_FLOOR).astype(jnp.bfloat16)
    mask = mask.transpose(1, 2, 0, 3).reshape(reqs, pairs, 2 * steps, blocks)
    expand = (np.arange(tokens)[None, :] // BLOCK == np.arange(blocks)[:, None]).astype(
        jnp.bfloat16
    )

    def whole(shape):
        return pl.BlockSpec(shape, lambda r: (0,) * len(shape))

    def per_request(shape):
        return pl.BlockSpec((1,) + shape, lambda r: (r,) + (0,) * len(shape))

    lanes = reqs * part
    partial, stats = pl.pallas_call(
        functools.partial(attend_kernel, steps, head_dim),
        grid=(reqs,),
        out_shape=(
            jax.ShapeDtypeStruct((2, groups, reqs, part, head_dim), jnp.bfloat16),
            jax.ShapeDtypeStruct((2, groups, 8, lanes), jnp.float32),
        ),
        in_specs=[
            pl.BlockSpec(memory_space=pltpu.SMEM),
            whole((2, head_dim)),
            whole((tokens, head_dim)),
            whole((tokens, head_dim)),
            whole((blocks, tokens)),
            per_request((pairs, rows, head_dim)),
            per_request((steps, wide)),
            per_request((steps, wide)),
            per_request((pairs, 2 * steps, blocks)),
            per_request((tokens, rank)),
            per_request((rank, wide)),
            per_request((tokens, wide)),
        ],
        out_specs=(
            pl.BlockSpec((2, groups, 1, part, head_dim), lambda r: (0, 0, r, 0, 0)),
            whole((2, groups, 8, lanes)),
        ),
        scratch_shapes=[pltpu.VMEM((tokens, head_dim), jnp.float32)] * 2,
        compiler_params=pltpu.CompilerParams(vmem_limit_bytes=40 * 2**20),
        name="attend",
    )(
        me.reshape(1).astype(jnp.int32), base, cos_off, sin_off, expand, q_rot, new_rot, new_val,
        mask, key_factors, key_basis, values,
    )
    rows_dev = reqs * heads_dev * steps
    partial = partial.reshape(2, groups, reqs, chips_group, heads_dev * steps, head_dim)
    partial = partial.transpose(0, 1, 3, 2, 4, 5).reshape(2, chips, rows_dev, head_dim)
    stats = stats.reshape(2, groups, 8, reqs, chips_group, heads_dev * steps)
    stats = stats.transpose(0, 1, 4, 2, 3, 5).reshape(2, chips, 8, rows_dev)

    width = out_weight.shape[1] // devices
    out_rows = reqs * steps
    dma = pltpu.SemaphoreType.DMA
    vmem = pl.BlockSpec(memory_space=pltpu.VMEM)
    out = pl.pallas_call(
        functools.partial(combine_kernel, chips, reqs, steps),
        out_shape=jax.ShapeDtypeStruct((out_rows, width), jnp.bfloat16),
        in_specs=[vmem, vmem, pl.BlockSpec(memory_space=pl.ANY)],
        out_specs=vmem,
        scratch_shapes=[pltpu.VMEM(out_weight.shape, out_weight.dtype)]
        + [
            pltpu.VMEM((chips, rows_dev, head_dim), jnp.bfloat16),
            pltpu.VMEM((chips, 8, rows_dev), jnp.float32),
        ]
        * 3
        + [pltpu.VMEM((chips, out_rows, width), jnp.bfloat16)] * 4
        + [dma]
        + [dma((chips,))] * 12,
        compiler_params=pltpu.CompilerParams(
            collective_id=0, has_side_effects=True, vmem_limit_bytes=40 * 2**20
        ),
        name="combine",
    )(partial, stats, out_weight)
    return out.reshape(reqs, steps, width).transpose(1, 0, 2)


def solution(mesh):
    placed = (
        P(None, "parts", None, None),
        P(None, "parts", None, None),
        P(None, "parts", None, None),
        P("parts", "store", None),
        P("parts", None, None),
        P("parts", "store", None),
        P(None, "parts", None, None),
        P(None, "parts", None),
        P("store", None),
    )
    return jax.shard_map(
        per_device, mesh=mesh, in_specs=placed, out_specs=P(None, "parts", "store"), check_vma=False
    )
```

profile of v0, /device:TPU:0, one launch (start us, length us, event | category | flops | bytes accessed | tf_op | source)
XLA Modules:
  0.0 51.5 jit_solution(2300849779431377426)
XLA Ops:
  0.0 0.0 copy-start.9
  0.0 0.0 copy-start.10
  0.0 0.0 copy-start.3
  0.0 0.0 copy-start.5
  0.0 0.0 copy-start.8
  0.0 0.0 copy-start.6
  0.0 0.0 copy-start.7
  0.0 0.0 copy-start.11
  0.0 0.0 copy-start.2
  0.1 0.8 %dynamic-slice_bitcast_fusion.base_ref = f32[2,128]{1,0:T(2,128)S(1)} fusion(f32[16,2,128]{2,1,0:T(2,128)} %constant.32.clone, s32[]{:T(128)S(6)} %select_n.14), kind=kLoop, calls=%fused_computation.16 | loop fusion | bytes 2052 | tf_op jit(solution)/shard_map/jit(dynamic_index_in_dim)/squeeze | solution.py:309
  0.9 1.5 %fusion.7 = (f32[8,4,64,64]{3,2,1,0:T(8,128)S(1)}, f32[8,4,64,64]{3,2,1,0:T(8,128)S(1)}) fusion(bf16[8,4,64,128]{3,2,1,0:T(8,128)(2,1)} %param.15), kind=kLoop, calls=%fused_computation.17 | loop fusion | bytes 2097152 | tf_op jit(solution)/shard_map/slice | solution.py:39
  2.4 1.5 %fusion.2 = bf16[8,4,64,128]{3,2,1,0:T(8,128)(2,1)S(1)} fusion(f32[8,4,64,64]{3,2,1,0:T(8,128)S(1)} %get-tuple-element.10, f32[8,4,64,64]{3,2,1,0:T(8,128)S(1)} %get-tuple-element.9, f32[8,128]{1,0:T(8,128)} %constant.39, f32[8,128]{1,0:T(8,128)} %constant.38, bf16[8,4,64,128]{3,2,1,0:T(8,128)(2,1)} %param.15), kind=kLoop, calls=%fused_computation.4 | loop fusion | flops 1572864 | bytes 2105344 | tf_op jit(solution)/shard_map/convert_element_type | solution.py:313
  3.9 0.6 %copy.21 = bf16[8,4,8,1,2,4,128]{6,0,5,4,2,1,3:T(8,128)(2,1)S(1)} copy(bf16[8,4,8,1,2,4,128]{6,5,4,2,1,0,3:T(4,128)(2,1)S(1)} %bitcast.26) | data formatting | bytes 1048576 | tf_op jit(solution)/shard_map/reshape | solution.py:315
  4.5 0.0 copy-done.6
  4.5 0.1 fusion.8
  4.6 0.0 copy-done.9
  4.6 0.0 copy-done.10
  4.6 0.1 fusion.6
  4.7 0.0 copy-done.8
  4.8 0.0 copy-done.7
  4.8 0.0 copy-done.11
  4.8 0.1 subtract_select_fusion
  4.9 4.4 %fusion = pred[8,4,8,64]{3,2,1,0:T(8,128)(4,1)S(1)} fusion(s32[8,4,8,64]{3,2,1,0:T(8,128)S(1)} %subtract_select_fusion), kind=kLoop, calls=%fused_computation.1 | loop fusion | flops 2080768 | bytes 81920 | tf_op jit(solution)/shard_map/reduce_or | solution.py:321
  9.4 1.4 %copy.25.factor_ref = bf16[4,512,160]{2,1,0:T(8,128)(2,1)S(1)} copy(bf16[4,512,160]{1,2,0:T(8,128)(2,1)} %param.18) | data formatting | bytes 1310720 | tf_op args[3]
  10.8 0.0 copy-done.3
  10.8 0.0 copy-done.5
  10.9 0.0 copy-done.2
  10.9 0.0 copy-start.1
  10.9 2.2 %copy-done.1 = bf16[4,512,1024]{2,1,0:T(8,128)(2,1)S(1)} copy-done((bf16[4,512,1024]{2,1,0:T(8,128)(2,1)S(1)}, bf16[4,512,1024]{2,1,0:T(8,128)(2,1)}, u32[]{:S(2)}) %copy-start.1) | copy-done | bytes 4194328
  13.1 0.0 copy-start.4
  13.1 0.9 %copy-done.4 = f32[512,128]{1,0:T(8,128)S(1)} copy-done((f32[512,128]{1,0:T(8,128)S(1)}, f32[512,128]{1,0:T(8,128)}, u32[]{:S(2)}) %copy-start.4) | copy-done | bytes 262168
  14.0 8.5 %attend.1 = (bf16[2,8,4,32,128]{4,3,2,1,0:T(8,128)(2,1)S(1)}, f32[2,8,8,128]{3,2,1,0:T(8,128)S(1)}) custom-call(s32[1]{0:T(128)} %bitcast.me_ref, f32[2,128]{1,0:T(2,128)S(1)} %dynamic-slice_bitcast_fusion.base_ref, f32[512,128]{1,0:T(8,128)S(1)} %copy-done.3, f32[512,128]{1,0:T(8,128)S(1)} %copy-done.4, bf16[64,512]{1,0:T(8,128)(2,1)S(1)} %copy-done.5, ...), custom_call_target="tpu_custom_call" | custom-call | tf_op jit(solution)/shard_map/attend/pallas_call | solution.py:335
  22.5 0.0 copy-start
  22.5 3.4 %copy-done = bf16[512,8192]{1,0:T(8,128)(2,1)S(1)} copy-done((bf16[512,8192]{1,0:T(8,128)(2,1)S(1)}, bf16[512,8192]{1,0:T(8,128)(2,1)}, u32[]{:S(2)}) %copy-start) | copy-done | bytes 8388632
  25.9 25.0 %combine.1 = bf16[32,512]{1,0:T(8,128)(2,1)S(1)} custom-call(bf16[2,8,128,128]{3,2,1,0:T(8,128)(2,1)S(1)} %bitcast.23, f32[2,8,8,128]{3,2,1,0:T(8,128)S(1)} %get-tuple-element.8.st_ref, bf16[512,8192]{1,0:T(8,128)(2,1)S(1)} %copy-done), custom_call_target="tpu_custom_call" | custom-call | tf_op jit(solution)/shard_map/combine/pallas_call | solution.py:377
  50.9 0.6 %copy.30 = bf16[4,8,512]{2,0,1:T(4,128)(2,1)} copy(bf16[4,8,512]{2,1,0:T(8,128)(2,1)S(1)} %bitcast.25) | data formatting | bytes 65536 | tf_op jit(solution)/shard_map/reshape | solution.py:396
  (3 shorter events, 0.1 us)
Async XLA Ops:
  0.0 4.6 %copy-start.9 = (f32[8,128]{1,0:T(8,128)S(1)}, f32[8,128]{1,0:T(8,128)}, u32[]{:S(2)}) copy-start(f32[8,128]{1,0:T(8,128)} %constant.39) | copy-start | bytes 12292
  0.0 4.6 %copy-start.10 = (f32[8,128]{1,0:T(8,128)S(1)}, f32[8,128]{1,0:T(8,128)}, u32[]{:S(2)}) copy-start(f32[8,128]{1,0:T(8,128)} %constant.38) | copy-start | bytes 12292
  0.0 10.8 %copy-start.3 = (f32[512,128]{1,0:T(8,128)S(1)}, f32[512,128]{1,0:T(8,128)}, u32[]{:S(2)}) copy-start(f32[512,128]{1,0:T(8,128)} %constant.35.clone.cos_ref) | copy-start | bytes 786436
  0.0 10.8 %copy-start.5 = (bf16[64,512]{1,0:T(8,128)(2,1)S(1)}, bf16[64,512]{1,0:T(8,128)(2,1)}, u32[]{:S(2)}) copy-start(bf16[64,512]{1,0:T(8,128)(2,1)} %constant.37.clone.expand_ref) | copy-start | bytes 196612
  0.0 4.7 %copy-start.8 = (bf16[8,4,8,128]{3,2,1,0:T(8,128)(2,1)S(1)}, bf16[8,4,8,128]{3,2,1,0:T(8,128)(2,1)}, u32[]{:S(2)}) copy-start(bf16[8,4,8,128]{3,2,1,0:T(8,128)(2,1)} %param.17) | copy-start | bytes 196612
  0.0 4.5 %copy-start.6 = (bf16[8,4,8,128]{3,2,1,0:T(8,128)(2,1)S(1)}, bf16[8,4,8,128]{3,2,1,0:T(8,128)(2,1)}, u32[]{:S(2)}) copy-start(bf16[8,4,8,128]{3,2,1,0:T(8,128)(2,1)} %param.16) | copy-start | bytes 196612
  0.0 4.8 %copy-start.7 = (s32[8,4,8,64]{3,2,1,0:T(8,128)S(1)}, s32[8,4,8,64]{3,2,1,0:T(8,128)}, u32[]{:S(2)}) copy-start(s32[8,4,8,64]{3,2,1,0:T(8,128)} %param.21) | copy-start | bytes 196612
  0.0 4.8 %copy-start.11 = (s32[8,4,8]{2,1,0:T(4,128)S(1)}, s32[8,4,8]{2,1,0:T(4,128)}, u32[]{:S(2)}) copy-start(s32[8,4,8]{2,1,0:T(4,128)} %param.22) | copy-start | bytes 3076
  0.0 10.8 %copy-start.2 = (bf16[4,160,1024]{2,1,0:T(8,128)(2,1)S(1)}, bf16[4,160,1024]{2,1,0:T(8,128)(2,1)}, u32[]{:S(2)}) copy-start(bf16[4,160,1024]{2,1,0:T(8,128)(2,1)} %basis_ref.1) | copy-start | bytes 3932164
  10.9 2.2 %copy-start.1 = (bf16[4,512,1024]{2,1,0:T(8,128)(2,1)S(1)}, bf16[4,512,1024]{2,1,0:T(8,128)(2,1)}, u32[]{:S(2)}) copy-start(bf16[4,512,1024]{2,1,0:T(8,128)(2,1)} %value_ref.1) | copy-start | bytes 12582916
  13.1 0.9 %copy-start.4 = (f32[512,128]{1,0:T(8,128)S(1)}, f32[512,128]{1,0:T(8,128)}, u32[]{:S(2)}) copy-start(f32[512,128]{1,0:T(8,128)} %constant.36.clone.sin_ref) | copy-start | bytes 786436
  22.5 3.4 %copy-start = (bf16[512,8192]{1,0:T(8,128)(2,1)S(1)}, bf16[512,8192]{1,0:T(8,128)(2,1)}, u32[]{:S(2)}) copy-start(bf16[512,8192]{1,0:T(8,128)(2,1)} %w_ref.1) | copy-start | bytes 25165828
where the time goes:
time: 51.8 us; the launch traced here: 51.5 us
  Pallas kernels  33.5 us (65%)
  local copies, waits for them, and re-layouts  11.7 us (23%)
  other arithmetic  6.14 us (12%)
    pallas_call x1, Pallas kernels, per_device(): pl.pallas_call(functools.partial(combine_kernel, chips, reqs, steps), out...  25 us
    pallas_call x1, Pallas kernels, per_device(): pl.pallas_call(functools.partial(attend_kernel, steps, head_dim), grid=(r...  8.52 us
    unnamed x25, local copies, waits for them, and re-layouts  7.96 us
    reduce_or x1, other arithmetic, per_device(): jnp.any(local[..., None, :] == jnp.arange(blocks, dtype=jnp.int32)[:, Non...  4.44 us
    slice x2, local copies, waits for them, and re-layouts, rotate(): swapped = jnp.concatenate([x[..., half:], x[..., :half]], axis=-1)  1.59 us
    convert_element_type x1, other arithmetic, per_device(): rotate(queries.astype(jnp.float32), cos_new, sin_new).astype(jnp.bfloat16)  1.46 us

commit v1 on v0

v1 whole, which is shorter than its diff:
```python
import functools
import math

import jax
import jax.numpy as jnp
import numpy as np
from jax import lax
from jax.experimental import pallas as pl
from jax.experimental.pallas import tpu as pltpu
from jax.sharding import PartitionSpec as P

BLOCK = 8
ROPE_THETA = 500000.0
NEG_FLOOR = -1e30
MESH = pl.DeviceIdType.MESH


def rope_freqs(head_dim):
    exponent = np.arange(head_dim // 2, dtype=np.float64) * (2.0 / head_dim)
    base = np.power(ROPE_THETA, -exponent)
    wavelength = 2.0 * math.pi / base
    smooth = (8192.0 / wavelength - 1.0) / 3.0
    middle = (1.0 - smooth) * base / 8.0 + smooth * base
    freqs = np.where(wavelength < 2048.0, base, np.where(wavelength > 8192.0, base / 8.0, middle))
    return freqs.astype(np.float32).astype(np.float64)


def rope_tables(positions, head_dim):
    angles = positions[:, None].astype(np.float64) * rope_freqs(head_dim)[None, :]
    cosine, sine = np.cos(angles), np.sin(angles)
    return (
        np.concatenate([cosine, cosine], -1).astype(np.float32),
        np.concatenate([sine, sine], -1).astype(np.float32),
    )


def attend_kernel(
    steps, head_dim, base_ref, cos_ref, sin_ref, new_cos_ref, new_sin_ref, expand_ref, x_ref,
    list_ref, factor_ref, basis_ref, value_ref, send_ref, keep_ref, stat_ref, cos_s, sin_s,
):
    r = pl.program_id(0)
    me = lax.axis_index("store")
    core = me % 2
    tokens = value_ref.shape[1]
    groups = value_ref.shape[2] // head_dim
    n_heads = x_ref.shape[1] - 2 * groups
    group = n_heads // groups
    blocks = expand_ref.shape[0]
    slots = list_ref.shape[2]
    half = group * steps
    part = half // 2
    rows = 2 * half
    wide = 2 * head_dim
    turn = head_dim // 2
    scale = head_dim ** -0.5
    lanes = stat_ref.shape[3]

    @pl.when(r == 0)
    def _():
        sign = jnp.where(
            lax.broadcasted_iota(jnp.int32, (tokens, head_dim), 1) < turn, -1.0, 1.0
        )
        base = base_ref[me]
        base_cos, base_sin = base[0:1], base[1:2]
        c, s = cos_ref[...], sin_ref[...]
        cos_s[...] = base_cos * c - base_sin * s
        sin_s[...] = (base_sin * c + base_cos * s) * sign
        stat_ref[...] = jnp.zeros_like(stat_ref)

    listed = list_ref[0].astype(jnp.float32).T
    block_ids = (
        lax.broadcasted_iota(jnp.int32, (blocks, groups * steps), 0) + me * blocks
    ).astype(jnp.float32)
    mask = jnp.full((blocks, groups * steps), NEG_FLOOR, jnp.float32)
    for j in range(slots):
        mask = jnp.where(listed[j : j + 1] == block_ids, 0.0, mask)
    bias_all = lax.dot_general(
        mask.astype(jnp.bfloat16), expand_ref[...], (((0,), (0,)), ((), ())),
        preferred_element_type=jnp.float32,
    )

    heads = x_ref[0, : n_heads + groups].astype(jnp.float32)
    heads = heads.reshape((n_heads + groups) * steps, head_dim)
    count = n_heads + groups
    swapped = pltpu.roll(heads, turn, 1).reshape(count, steps, head_dim)
    turned = heads.reshape(count, steps, head_dim) * new_cos_ref[...] + swapped * new_sin_ref[...]
    q_all = turned[:n_heads].reshape(n_heads * steps, head_dim).astype(jnp.bfloat16)
    nk_all = turned[n_heads:]
    nv_all = x_ref[0, n_heads + groups :].astype(jnp.float32)

    cosine, sine = cos_s[...], sin_s[...]
    step_of = lax.broadcasted_iota(jnp.int32, (rows, steps), 0) % steps
    fresh_ok = (lax.broadcasted_iota(jnp.int32, (rows, steps), 1) <= step_of) & (me == 0)
    spot = lax.broadcasted_iota(jnp.int32, (part, lanes), 1) == (
        lax.broadcasted_iota(jnp.int32, (part, lanes), 0) + r * part
    )
    contract = (((1,), (1,)), ((), ()))
    zero = jnp.zeros((half, head_dim), jnp.bfloat16)
    for p in range(groups // 2):
        cols = slice(p * wide, (p + 1) * wide)
        keys = lax.dot_general(
            factor_ref[0], basis_ref[0, :, cols], (((0,), (0,)), ((), ())),
            preferred_element_type=jnp.float32,
        )
        keys = jnp.concatenate(
            [
                (k * cosine + pltpu.roll(k, turn, 1) * sine).astype(jnp.bfloat16)
                for k in (keys[:, :head_dim], keys[:, head_dim:])
            ],
            axis=1,
        )
        q = q_all[p * rows : (p + 1) * rows]
        q = jnp.concatenate(
            [jnp.concatenate([q[:half], zero], 1), jnp.concatenate([zero, q[half:]], 1)], 0
        )
        nk = jnp.concatenate([nk_all[2 * p], nk_all[2 * p + 1]], 1).astype(jnp.bfloat16)
        nv = jnp.concatenate([nv_all[2 * p], nv_all[2 * p + 1]], 1).astype(jnp.bfloat16)
        scores = lax.dot_general(q, keys, contract, preferred_element_type=jnp.float32) * scale
        bias = bias_all[p * 2 * steps : (p + 1) * 2 * steps]
        scores = (
            scores.reshape(2, group, steps, tokens) + bias.reshape(2, 1, steps, tokens)
        ).reshape(rows, tokens)
        fresh = lax.dot_general(q, nk, contract, preferred_element_type=jnp.float32) * scale
        fresh = jnp.where(fresh_ok, fresh, NEG_FLOOR)
        top = jnp.maximum(
            jnp.max(scores, axis=1, keepdims=True), jnp.max(fresh, axis=1, keepdims=True)
        )
        weights = jnp.exp(scores - top)
        fresh = jnp.exp(fresh - top)
        total = jnp.sum(weights, axis=1, keepdims=True) + jnp.sum(fresh, axis=1, keepdims=True)

        def split_dot(w, v):
            high = w.astype(jnp.bfloat16)
            low = (w - high.astype(jnp.float32)).astype(jnp.bfloat16)
            both = jnp.dot(
                jnp.concatenate([high, low], 0), v, preferred_element_type=jnp.float32
            )
            return both[:rows] + both[rows:]

        out = split_dot(weights, value_ref[0, :, cols]) + split_dot(fresh, nv)
        for u in range(2):
            g = 2 * p + u
            mine = out[u * half : (u + 1) * half, u * head_dim : (u + 1) * head_dim]
            keep_ref[g, 0] = jnp.where(core == 0, mine[:part], mine[part:])
            send_ref[g, 0] = jnp.where(core == 0, mine[part:], mine[:part]).astype(jnp.bfloat16)
            for c in range(2):
                at = u * half + c * part
                for i, column in enumerate((top, total)):
                    stat_ref[c, i, g : g + 1] += jnp.sum(
                        jnp.where(spot, column[at : at + part], 0.0), axis=0, keepdims=True
                    )


def combine_kernel(
    chips, reqs, steps, send_ref, keep_ref, st_ref, w_ref, out_ref, w_s, o1, sts, own_w, twin_w,
    o2s, o2r, t1s, t1r, t2s, t2r, w_sem, s_o1, r_o1, s_st, r_st, s_o2, r_o2, s_t1, r_t1, s_t2,
    r_t2,
):
    me = lax.axis_index("store")
    chip, core = me // 2, me % 2
    twin = chip * 2 + 1 - core
    devices = 2 * chips
    rows = send_ref.shape[1]
    head_dim = send_ref.shape[2]
    heads = rows // (reqs * steps)
    width = out_ref.shape[1]

    weight_copy = pltpu.make_async_copy(w_ref, w_s, w_sem)
    weight_copy.start()

    def chip_at(i):
        return lax.rem(chip + i, chips)

    def device_at(i):
        return lax.rem(me + i, devices)

    def remote(src, dst, send, recv, device):
        return pltpu.make_async_remote_copy(
            src_ref=src, dst_ref=dst, send_sem=send, recv_sem=recv,
            device_id={"store": device}, device_id_type=MESH,
        )

    barrier = pltpu.get_barrier_semaphore()

    def greet(i, carry):
        pl.semaphore_signal(
            barrier, inc=1, device_id={"store": device_at(i)}, device_id_type=MESH
        )
        return carry

    lax.fori_loop(1, devices, greet, 0)
    pl.semaphore_wait(barrier, devices - 1)

    first = remote(send_ref, o1, s_o1, r_o1, twin)

    def gather(d, slot):
        return remote(st_ref.at[lax.rem(d, 2)], sts.at[slot], s_st.at[d], r_st.at[slot], d)

    def second(k, slot):
        return remote(o2s.at[k], o2r.at[slot], s_o2.at[k], r_o2.at[slot], k * 2 + core)

    def third(k):
        return remote(t1s.at[k], t1r.at[k], s_t1.at[k], r_t1.at[k], twin)

    def fourth(k, slot):
        return remote(t2s.at[k], t2r.at[slot], s_t2.at[k], r_t2.at[slot], k * 2 + core)

    def send_stats(i, carry):
        gather(device_at(i), me).start()
        return carry

    lax.fori_loop(1, devices, send_stats, 0)
    first.start()
    sts[me] = st_ref[core]

    def wait_stats(i, carry):
        d = device_at(i)
        gather(d, d).wait_recv()
        return carry

    lax.fori_loop(1, devices, wait_stats, 0)
    top = sts[0, 0]
    for d in range(1, devices):
        top = jnp.maximum(top, sts[d, 0])
    total = jnp.exp(sts[0, 0] - top) * sts[0, 1]
    for d in range(1, devices):
        total = total + jnp.exp(sts[d, 0] - top) * sts[d, 1]
    columns = jnp.concatenate(
        [jnp.exp(sts[me, 0] - top) / total, jnp.exp(sts[twin, 0] - top) / total], 0
    ).T
    for k in range(chips):
        own_w[k] = jnp.broadcast_to(columns[:, k : k + 1], (rows, head_dim))
        twin_w[k] = jnp.broadcast_to(columns[:, chips + k : chips + k + 1], (rows, head_dim))
    first.wait_recv()

    def merged(k):
        return keep_ref[k] * own_w[k] + o1[k].astype(jnp.float32) * twin_w[k]

    def send_second(i, carry):
        k = chip_at(i)
        o2s[k] = merged(k).astype(jnp.bfloat16)
        second(k, chip).start()
        return carry

    lax.fori_loop(1, chips, send_second, 0)

    def add_second(i, attn):
        k = chip_at(i)
        second(k, k).wait_recv()
        return attn + o2r[k].astype(jnp.float32)

    attn = lax.fori_loop(1, chips, add_second, merged(chip))
    flat = jnp.concatenate(
        [
            jnp.concatenate(
                [
                    attn[(r * heads + j) * steps : (r * heads + j + 1) * steps]
                    for r in range(reqs)
                ],
                0,
            )
            for j in range(heads)
        ],
        1,
    ).astype(jnp.bfloat16)
    weight_copy.wait()

    def term(k, which):
        at = pl.multiple_of((2 * k + which) * width, width)
        return jnp.dot(flat, w_s[:, pl.ds(at, width)], preferred_element_type=jnp.float32)

    def send_third(i, carry):
        k = chip_at(i)
        t1s[k] = term(k, 1 - core).astype(jnp.bfloat16)
        third(k).start()
        return carry

    lax.fori_loop(1, chips + 1, send_third, 0)

    def summed(k):
        mine = term(k, core)
        third(k).wait_recv()
        return mine + t1r[k].astype(jnp.float32)

    def send_fourth(i, carry):
        k = chip_at(i)
        t2s[k] = summed(k).astype(jnp.bfloat16)
        fourth(k, chip).start()
        return carry

    lax.fori_loop(1, chips, send_fourth, 0)
    own = summed(chip)

    def add_fourth(i, total):
        k = chip_at(i)
        fourth(k, k).wait_recv()
        return total + t2r[k].astype(jnp.float32)

    out_ref[...] = lax.fori_loop(1, chips, add_fourth, own).astype(out_ref.dtype)

    def drain(i, carry):
        k = chip_at(i)
        for copy in (second(k, k), third(k), fourth(k, k)):
            copy.wait_send()
        return carry

    def drain_stats(i, carry):
        gather(device_at(i), me).wait_send()
        return carry

    lax.fori_loop(1, chips, drain, 0)
    lax.fori_loop(1, devices, drain_stats, 0)
    first.wait_send()
    third(chip).wait_send()


def per_device(
    queries, new_keys, new_values, key_factors, key_basis, values, block_index, block_count,
    out_weight,
):
    devices = lax.axis_size("store")
    chips = devices // 2
    steps, reqs, n_heads, head_dim = queries.shape
    groups = new_keys.shape[2]
    group = n_heads // groups
    tokens = values.shape[1]
    rank = key_factors.shape[2]
    blocks = tokens // BLOCK
    heads_dev = n_heads // devices
    slots = block_index.shape[-1]
    half_group = group // 2
    part = half_group * steps
    wide = groups * head_dim
    chips_group = half_group // heads_dev

    cos_off, sin_off = rope_tables(np.arange(tokens), head_dim)
    base = np.stack(rope_tables(np.arange(devices) * tokens, head_dim), 1)
    sign = np.where(np.arange(head_dim) < head_dim // 2, -1.0, 1.0).astype(np.float32)
    cos_new, sin_new = rope_tables(tokens * devices + np.arange(steps), head_dim)
    q = queries
    if chips_group > 1:
        q = q.reshape(steps, reqs, groups, chips_group, 2, heads_dev, head_dim)
        q = q.swapaxes(3, 4).reshape(queries.shape)
    x = jnp.concatenate([q, new_keys, new_values], axis=2).transpose(1, 2, 0, 3)
    lists = jnp.where(
        jnp.arange(slots, dtype=jnp.int32) < block_count[..., None], block_index, -1
    )
    lists = lists.transpose(1, 2, 0, 3).reshape(reqs, groups * steps, slots)
    expand = (np.arange(tokens)[None, :] // BLOCK == np.arange(blocks)[:, None]).astype(
        jnp.bfloat16
    )

    def whole(shape):
        return pl.BlockSpec(shape, lambda r: (0,) * len(shape))

    def per_request(shape):
        return pl.BlockSpec((1,) + shape, lambda r: (r,) + (0,) * len(shape))

    lanes = reqs * part
    out_block = pl.BlockSpec((groups, 1, part, head_dim), lambda r: (0, r, 0, 0))
    send, keep, stats = pl.pallas_call(
        functools.partial(attend_kernel, steps, head_dim),
        grid=(reqs,),
        out_shape=(
            jax.ShapeDtypeStruct((groups, reqs, part, head_dim), jnp.bfloat16),
            jax.ShapeDtypeStruct((groups, reqs, part, head_dim), jnp.float32),
            jax.ShapeDtypeStruct((2, 2, groups, lanes), jnp.float32),
        ),
        in_specs=[
            whole((devices, 2, head_dim)),
            whole((tokens, head_dim)),
            whole((tokens, head_dim)),
            whole((steps, head_dim)),
            whole((steps, head_dim)),
            whole((blocks, tokens)),
            per_request((n_heads + 2 * groups, steps, head_dim)),
            per_request((groups * steps, slots)),
            per_request((rank, tokens)),
            per_request((rank, wide)),
            per_request((tokens, wide)),
        ],
        out_specs=(out_block, out_block, whole((2, 2, groups, lanes))),
        scratch_shapes=[pltpu.VMEM((tokens, head_dim), jnp.float32)] * 2,
        compiler_params=pltpu.CompilerParams(vmem_limit_bytes=60 * 2**20),
        name="attend",
    )(
        base, cos_off, sin_off, cos_new, sin_new * sign, expand, x, lists,
        key_factors.swapaxes(1, 2), key_basis, values,
    )
    rows_dev = reqs * heads_dev * steps

    def by_chip(y):
        y = y.reshape(groups, reqs, chips_group, heads_dev * steps, head_dim)
        return y.transpose(0, 2, 1, 3, 4).reshape(chips, rows_dev, head_dim)

    stats = stats.reshape(2, 2, groups, reqs, chips_group, heads_dev * steps)
    stats = stats.transpose(0, 1, 2, 4, 3, 5).reshape(2, 2, chips, rows_dev)

    width = out_weight.shape[1] // devices
    out_rows = reqs * steps
    dma = pltpu.SemaphoreType.DMA
    vmem = pl.BlockSpec(memory_space=pltpu.VMEM)
    out = pl.pallas_call(
        functools.partial(combine_kernel, chips, reqs, steps),
        out_shape=jax.ShapeDtypeStruct((out_rows, width), jnp.bfloat16),
        in_specs=[vmem, vmem, vmem, pl.BlockSpec(memory_space=pl.ANY)],
        out_specs=vmem,
        scratch_shapes=[
            pltpu.VMEM(out_weight.shape, out_weight.dtype),
            pltpu.VMEM((chips, rows_dev, head_dim), jnp.bfloat16),
            pltpu.VMEM((devices, 2, chips, rows_dev), jnp.float32),
            pltpu.VMEM((chips, rows_dev, head_dim), jnp.float32),
            pltpu.VMEM((chips, rows_dev, head_dim), jnp.float32),
            pltpu.VMEM((chips, rows_dev, head_dim), jnp.bfloat16),
            pltpu.VMEM((chips, rows_dev, head_dim), jnp.bfloat16),
        ]
        + [pltpu.VMEM((chips, out_rows, width), jnp.bfloat16)] * 4
        + [dma, dma, dma, dma((devices,)), dma((devices,))]
        + [dma((chips,))] * 6,
        compiler_params=pltpu.CompilerParams(
            collective_id=0, has_side_effects=True, vmem_limit_bytes=60 * 2**20
        ),
        name="combine",
    )(by_chip(send), by_chip(keep), stats, out_weight)
    return out.reshape(reqs, steps, width).transpose(1, 0, 2)


def solution(mesh):
    placed = (
        P(None, "parts", None, None),
        P(None, "parts", None, None),
        P(None, "parts", None, None),
        P("parts", "store", None),
        P("parts", None, None),
        P("parts", "store", None),
        P(None, "parts", None, None),
        P(None, "parts", None),
        P("store", None),
    )
    return jax.shard_map(
        per_device, mesh=mesh, in_specs=placed, out_specs=P(None, "parts", "store"), check_vma=False
    )
```

time: 51.8 us -> 51.2 us (0.988)
  Pallas kernels: 33.5 us -> 43.6 us
  local copies, waits for them, and re-layouts: 11.7 us -> 5.26 us
  other arithmetic: 6.14 us -> 1.94 us
    pallas_call x1, Pallas kernels: 25 us -> 30.1 us  [per_device(): pl.pallas_call(functools.partial(combine_kernel, chips, reqs, steps), out...]
    pallas_call x1, Pallas kernels: 8.52 us -> 13.5 us  [per_device(): pl.pallas_call(functools.partial(attend_kernel, steps, head_dim), grid=(r...]
    unnamed x25 -> x3, local copies, waits for them, and re-layouts: 7.96 us -> 3.12 us
    reduce_or x1 -> x0, other arithmetic: 4.44 us -> none  [per_device(): jnp.any(local[..., None, :] == jnp.arange(blocks, dtype=jnp.int32)[:, Non...]
    transpose x1 -> x2, other arithmetic: 0.11 us -> 1.94 us  [the longest x1 1.01 us: per_device(): lists = lists.transpose(1, 2, 0, 3).reshape(reqs, groups * steps, slots)]
    slice x2 -> x0, local copies, waits for them, and re-layouts: 1.59 us -> none  [rotate(): swapped = jnp.concatenate([x[..., half:], x[..., :half]], axis=-1)]
    convert_element_type x2 -> x0, other arithmetic: 1.48 us -> none  [the longest x1 1.46 us: per_device(): rotate(queries.astype(jnp.float32), cos_new, sin_new).astype(jnp.bfloat16)]
    squeeze x1 -> x0, local copies, waits for them, and re-layouts: 0.82 us -> none  [per_device(): lax.dynamic_index_in_dim(jnp.asarray(base_tab), me, 0, keepdims=False)]
where the time goes in v1:
time: 51.2 us; the launch traced here: 50.8 us
  Pallas kernels  43.6 us (85%)
  local copies, waits for them, and re-layouts  5.26 us (10%)
  other arithmetic  1.94 us (4%)
    pallas_call x1, Pallas kernels, per_device(): pl.pallas_call(functools.partial(combine_kernel, chips, reqs, steps), out...  30.1 us
    pallas_call x1, Pallas kernels, per_device(): pl.pallas_call(functools.partial(attend_kernel, steps, head_dim), grid=(r...  13.5 us
    unnamed x3, local copies, waits for them, and re-layouts  3.12 us
    reshape x1, local copies, waits for them, and re-layouts, per_device(): return out.reshape(reqs, steps, width).transpose(1, 0, 2)  1.39 us

profile of v1, /device:TPU:0, one launch (start us, length us, event | category | flops | bytes accessed | tf_op | source)
XLA Modules:
  0.0 50.8 jit_solution(17614075630976774192)
XLA Ops:
  0.0 0.9 %copy.17 = bf16[8,4,8,128]{3,0,2,1:T(8,128)(2,1)S(1)} copy(bf16[8,4,8,128]{3,2,1,0:T(8,128)(2,1)} %param.16) | data formatting | bytes 131072 | tf_op args[1]
  0.9 0.9 %copy.18 = bf16[8,4,8,128]{3,0,2,1:T(8,128)(2,1)S(1)} copy(bf16[8,4,8,128]{3,2,1,0:T(8,128)(2,1)} %param.17) | data formatting | bytes 131072 | tf_op args[2]
  1.7 1.0 %select_bitcast_fusion = s32[4,8,8,64]{3,1,0,2:T(8,128)S(1)} fusion(s32[8,4,8,64]{3,2,1,0:T(8,128)} %param.21, s32[8,4,8]{2,1,0:T(4,128)} %param.22), kind=kLoop, calls=%fused_computation.2 | loop fusion | flops 32768 | bytes 132096 | tf_op jit(solution)/shard_map/transpose | solution.py:348
  2.8 0.7 %copy.23 = s32[4,8,8,64]{3,2,1,0:T(8,128)} copy(s32[4,8,8,64]{3,1,0,2:T(8,128)S(1)} %select_bitcast_fusion) | data formatting | bytes 131072 | tf_op jit(solution)/shard_map/transpose | solution.py:348
  3.5 1.4 %copy.16 = bf16[8,4,64,128]{3,0,2,1:T(8,128)(2,1)S(1)} copy(bf16[8,4,64,128]{3,2,1,0:T(8,128)(2,1)} %param.15) | data formatting | bytes 1048576 | tf_op args[0]
  4.9 0.9 %maximum_bitcast_fusion.x_ref = bf16[4,80,8,128]{3,2,1,0:T(8,128)(2,1)} fusion(bf16[8,4,8,128]{3,0,2,1:T(8,128)(2,1)S(1)} %copy.18, bf16[8,4,8,128]{3,0,2,1:T(8,128)(2,1)S(1)} %copy.17, bf16[8,4,64,128]{3,0,2,1:T(8,128)(2,1)S(1)} %copy.16), kind=kLoop, calls=%fused_computation | loop fusion | flops 655360 | bytes 1310720 | tf_op jit(solution)/shard_map/transpose | solution.py:344
  5.8 13.5 %attend.1 = (bf16[8,4,32,128]{3,2,1,0:T(8,128)(2,1)}, f32[8,4,32,128]{3,2,1,0:T(8,128)}, f32[2,2,8,128]{3,2,1,0:T(8,128)}) custom-call(f32[16,2,128]{2,1,0:T(2,128)} %constant.14.clone.base_ref, f32[512,128]{1,0:T(8,128)} %constant.15.clone.cos_ref, f32[512,128]{1,0:T(8,128)} %constant.16.clone.sin_ref, f32[8,128]{1,0:T(8,128)} %constant.17.clone.new_cos_ref, ...), custom_call_target="tpu_custom_call" | custom-call | tf_op jit(solution)/shard_map/attend/pallas_call | solution.py:361
  19.3 30.1 %combine.1 = bf16[32,512]{1,0:T(8,128)(2,1)} custom-call(bf16[8,128,128]{2,1,0:T(8,128)(2,1)} %bitcast.17, f32[8,128,128]{2,1,0:T(8,128)} %bitcast.16, f32[2,2,8,128]{3,2,1,0:T(8,128)} %get-tuple-element.10.st_ref, bf16[512,8192]{1,0:T(8,128)(2,1)} %w_ref.1), custom_call_target="tpu_custom_call" | custom-call | tf_op jit(solution)/shard_map/combine/pallas_call | solution.py:403
  49.4 1.4 %copy.24 = bf16[4,8,512]{2,0,1:T(4,128)(2,1)} copy(bf16[4,8,512]{2,1,0:T(8,128)(2,1)} %bitcast.18) | data formatting | bytes 65536 | tf_op jit(solution)/shard_map/reshape | solution.py:425

commit v2 on v1

v2 whole, which is shorter than its diff:
```python
import functools
import math

import jax
import jax.numpy as jnp
import numpy as np
from jax import lax
from jax.experimental import pallas as pl
from jax.experimental.pallas import tpu as pltpu
from jax.sharding import PartitionSpec as P

BLOCK = 8
ROPE_THETA = 500000.0
NEG_FLOOR = -1e30
MESH = pl.DeviceIdType.MESH


def rope_freqs(head_dim):
    exponent = np.arange(head_dim // 2, dtype=np.float64) * (2.0 / head_dim)
    base = np.power(ROPE_THETA, -exponent)
    wavelength = 2.0 * math.pi / base
    smooth = (8192.0 / wavelength - 1.0) / 3.0
    middle = (1.0 - smooth) * base / 8.0 + smooth * base
    freqs = np.where(wavelength < 2048.0, base, np.where(wavelength > 8192.0, base / 8.0, middle))
    return freqs.astype(np.float32).astype(np.float64)


def rope_tables(positions, head_dim):
    angles = positions[:, None].astype(np.float64) * rope_freqs(head_dim)[None, :]
    cosine, sine = np.cos(angles), np.sin(angles)
    return (
        np.concatenate([cosine, cosine], -1).astype(np.float32),
        np.concatenate([sine, sine], -1).astype(np.float32),
    )


def attend_kernel(
    steps, head_dim, head_order, place, base_ref, cos_ref, sin_ref, new_cos_ref, new_sin_ref,
    expand_ref, q_ref, nk_ref, nv_ref, list_ref, factor_ref, basis_ref, value_ref, send_ref,
    keep_ref, stat_ref, cos_s, sin_s, head_s, nv_s, bias_s,
):
    r = pl.program_id(0)
    me = lax.axis_index("store")
    core = me % 2
    tokens = value_ref.shape[1]
    groups = value_ref.shape[2] // head_dim
    n_heads = q_ref.shape[2]
    group = n_heads // groups
    blocks = expand_ref.shape[0]
    slots = list_ref.shape[3]
    half = group * steps
    part = half // 2
    rows = 2 * half
    wide = 2 * head_dim
    turn = head_dim // 2
    scale = head_dim ** -0.5
    lanes = stat_ref.shape[3]

    @pl.when(r == 0)
    def _():
        sign = jnp.where(
            lax.broadcasted_iota(jnp.int32, (tokens, head_dim), 1) < turn, -1.0, 1.0
        )
        base = base_ref[me]
        base_cos, base_sin = base[0:1], base[1:2]
        c, s = cos_ref[...], sin_ref[...]
        cos_s[...] = base_cos * c - base_sin * s
        sin_s[...] = (base_sin * c + base_cos * s) * sign
        stat_ref[...] = jnp.zeros_like(stat_ref)

    listed = list_ref[:, 0].reshape(steps * groups, slots).astype(jnp.float32).T
    block_ids = (
        lax.broadcasted_iota(jnp.int32, (blocks, groups * steps), 0) + me * blocks
    ).astype(jnp.float32)
    mask = jnp.full((blocks, groups * steps), NEG_FLOOR, jnp.float32)
    for j in range(slots):
        mask = jnp.where(listed[j : j + 1] == block_ids, 0.0, mask)
    bias_all = lax.dot_general(
        mask.astype(jnp.bfloat16), expand_ref[...], (((0,), (0,)), ((), ())),
        preferred_element_type=jnp.float32,
    )
    n_lists = groups * steps
    for c in range(tokens // head_dim):
        bias_s[c * n_lists : (c + 1) * n_lists] = bias_all[:, c * head_dim : (c + 1) * head_dim]

    count = n_heads + groups
    for t in range(steps):
        x = jnp.concatenate(
            [q_ref[t, 0].astype(jnp.float32), nk_ref[t, 0].astype(jnp.float32)], 0
        )
        head_s[t * count : (t + 1) * count] = (
            x * new_cos_ref[t : t + 1] + pltpu.roll(x, turn, 1) * new_sin_ref[t : t + 1]
        )
        nv_s[t * groups : (t + 1) * groups] = nv_ref[t, 0].astype(jnp.float32)

    def of_steps(ref, at, stride):
        return ref[pl.ds(at, steps, stride=stride)]

    cosine, sine = cos_s[...], sin_s[...]
    step_of = lax.broadcasted_iota(jnp.int32, (rows, steps), 0) % steps
    fresh_ok = (lax.broadcasted_iota(jnp.int32, (rows, steps), 1) <= step_of) & (me == 0)
    spot = lax.broadcasted_iota(jnp.int32, (part, lanes), 1) == (
        lax.broadcasted_iota(jnp.int32, (part, lanes), 0) + r * part
    )
    contract = (((1,), (1,)), ((), ()))
    zero = jnp.zeros((half, head_dim), jnp.bfloat16)
    keys_all = lax.dot_general(
        factor_ref[0], basis_ref[0], (((0,), (0,)), ((), ())), preferred_element_type=jnp.float32
    )
    for p in range(groups // 2):
        cols = slice(p * wide, (p + 1) * wide)
        keys = jnp.concatenate(
            [
                (k * cosine + pltpu.roll(k, turn, 1) * sine).astype(jnp.bfloat16)
                for k in (
                    keys_all[:, g * head_dim : (g + 1) * head_dim] for g in (2 * p, 2 * p + 1)
                )
            ],
            axis=1,
        )
        q = jnp.concatenate(
            [of_steps(head_s, h, count) for h in head_order[2 * p * group : 2 * (p + 1) * group]],
            0,
        ).astype(jnp.bfloat16)
        q = jnp.concatenate(
            [jnp.concatenate([q[:half], zero], 1), jnp.concatenate([zero, q[half:]], 1)], 0
        )
        nk = jnp.concatenate(
            [of_steps(head_s, n_heads + 2 * p + u, count) for u in range(2)], 1
        ).astype(jnp.bfloat16)
        nv = jnp.concatenate(
            [of_steps(nv_s, 2 * p + u, groups) for u in range(2)], 1
        ).astype(jnp.bfloat16)
        bias = jnp.concatenate(
            [
                jnp.concatenate(
                    [of_steps(bias_s, c * n_lists + 2 * p + u, groups) for u in range(2)], 0
                )
                for c in range(tokens // head_dim)
            ],
            1,
        )
        scores = lax.dot_general(q, keys, contract, preferred_element_type=jnp.float32) * scale
        scores = (
            scores.reshape(2, group, steps, tokens) + bias.reshape(2, 1, steps, tokens)
        ).reshape(rows, tokens)
        fresh = lax.dot_general(q, nk, contract, preferred_element_type=jnp.float32) * scale
        fresh = jnp.where(fresh_ok, fresh, NEG_FLOOR)
        top = jnp.maximum(
            jnp.max(scores, axis=1, keepdims=True), jnp.max(fresh, axis=1, keepdims=True)
        )
        weights = jnp.exp(scores - top)
        fresh = jnp.exp(fresh - top)
        total = jnp.sum(weights, axis=1, keepdims=True) + jnp.sum(fresh, axis=1, keepdims=True)

        def split_dot(w, v):
            high = w.astype(jnp.bfloat16)
            low = (w - high.astype(jnp.float32)).astype(jnp.bfloat16)
            both = jnp.dot(
                jnp.concatenate([high, low], 0), v, preferred_element_type=jnp.float32
            )
            return both[:rows] + both[rows:]

        out = split_dot(weights, value_ref[0, :, cols]) + split_dot(fresh, nv)
        for u in range(2):
            g = place[2 * p + u]
            mine = out[u * half : (u + 1) * half, u * head_dim : (u + 1) * head_dim]
            keep_ref[g, 0] = jnp.where(core == 0, mine[:part], mine[part:])
            send_ref[g, 0] = jnp.where(core == 0, mine[part:], mine[:part])
            for c in range(2):
                at = u * half + c * part
                for i, column in enumerate((top, total)):
                    stat_ref[c, i, g : g + 1] += jnp.sum(
                        jnp.where(spot, column[at : at + part], 0.0), axis=0, keepdims=True
                    )


def combine_kernel(
    chips, reqs, steps, send_ref, keep_ref, st_ref, w_ref, out_ref, w_s, o1, st1, weight_s, near,
    o2s, o2r, st2s, st2r, o3s, o3r, st3s, st3r, t1s, t1r, t2s, t2r, t3s, t3r, sem, k_sem, z_sem,
):
    me = lax.axis_index("store")
    chip, core = me // 2, me % 2
    lines = chips // 2
    line, side = chip // 2, chip % 2
    twin = chip * 2 + 1 - core
    mate = (line * 2 + 1 - side) * 2 + core
    rows = send_ref.shape[2]
    head_dim = send_ref.shape[3]
    heads = rows // (reqs * steps)
    width = out_ref.shape[1]

    weight_copy = pltpu.make_async_copy(w_ref, w_s, sem.at[0])
    weight_copy.start()

    def line_at(i):
        return lax.rem(line + i, lines)

    def device_of(z):
        return (z * 2 + side) * 2 + core

    def remote(src, dst, send, recv, device):
        return pltpu.make_async_remote_copy(
            src_ref=src, dst_ref=dst, send_sem=send, recv_sem=recv,
            device_id={"store": device}, device_id_type=MESH,
        )

    barrier = pltpu.get_barrier_semaphore()
    for device in (twin, mate):
        pl.semaphore_signal(barrier, inc=1, device_id={"store": device}, device_id_type=MESH)

    def greet(i, carry):
        pl.semaphore_signal(
            barrier, inc=1, device_id={"store": device_of(line_at(i))}, device_id_type=MESH
        )
        return carry

    lax.fori_loop(1, lines, greet, 0)
    pl.semaphore_wait(barrier, lines + 1)

    def loop(start, stop, step):
        def body(i, carry):
            step(line_at(i))
            return carry

        lax.fori_loop(start, stop, body, 0)

    stats_1 = remote(st_ref.at[1 - core], st1, sem.at[1], sem.at[2], twin)
    stats_2 = remote(st2s, st2r, sem.at[3], sem.at[4], mate)

    def first(which):
        return remote(
            send_ref.at[which], o1.at[which], k_sem.at[0, which], k_sem.at[1, which], twin
        )

    def second(z):
        return remote(o2s.at[z], o2r.at[z], z_sem.at[0, z], z_sem.at[1, z], mate)

    def third(z, slot):
        device = device_of(z)
        return (
            remote(st3s.at[z], st3r.at[slot], z_sem.at[2, z], z_sem.at[3, slot], device),
            remote(o3s.at[z], o3r.at[slot], z_sem.at[4, z], z_sem.at[5, slot], device),
        )

    def twin_term(which, z):
        at = which * lines + z
        return remote(t1s.at[at], t1r.at[at], k_sem.at[2, at], k_sem.at[3, at], twin)

    def mate_term(z):
        return remote(t2s.at[z], t2r.at[z], z_sem.at[6, z], z_sem.at[7, z], mate)

    def line_term(z, slot):
        return remote(
            t3s.at[z], t3r.at[slot], z_sem.at[8, z], z_sem.at[9, slot], device_of(z)
        )

    other = 1 - side
    stats_1.start()
    first(other).start()
    first(side).start()

    def join(a_top, a_sum, b_top, b_sum):
        top = jnp.maximum(a_top, b_top)
        a, b = jnp.exp(a_top - top), jnp.exp(b_top - top)
        return top, a * a_sum + b * b_sum, a, b

    def spread(at, columns):
        columns = columns.T
        for k in range(columns.shape[1]):
            weight_s[at + k] = jnp.broadcast_to(columns[:, k : k + 1], (rows, head_dim))

    stats_1.wait_recv()
    my_top, my_sum, a, b = join(st_ref[core, 0], st_ref[core, 1], st1[0], st1[1])

    def side_of(x, which):
        return jnp.where(which == 0, x[:lines], x[lines:])

    st2s[0], st2s[1] = side_of(my_top, other), side_of(my_sum, other)
    stats_2.start()
    spread(0, jnp.concatenate([a, b], 0))

    def joined(which, z):
        k = which * lines + z
        return keep_ref[which, z] * weight_s[k] + o1[which, z] * weight_s[chips + k]

    first(other).wait_recv()

    def send_second(z):
        o2s[z] = joined(other, z).astype(jnp.bfloat16)
        second(z).start()

    loop(1, lines + 1, send_second)
    stats_2.wait_recv()
    near_top, near_sum, a, b = join(
        side_of(my_top, side), side_of(my_sum, side), st2r[0], st2r[1]
    )
    pad = jnp.zeros((6, rows), jnp.float32)
    for z in range(lines):
        st3s[z] = jnp.concatenate([near_top[z : z + 1], near_sum[z : z + 1], pad], 0)
    st3r[line] = st3s[line]
    loop(1, lines, lambda z: third(z, line)[0].start())
    first(side).wait_recv()
    for z in range(lines):
        near[z] = joined(side, z)
    spread(0, jnp.concatenate([a, b], 0))

    def paired(z):
        second(z).wait_recv()
        return near[z] * weight_s[z] + o2r[z].astype(jnp.float32) * weight_s[lines + z]

    def send_third(z):
        o3s[z] = paired(z).astype(jnp.bfloat16)
        third(z, line)[1].start()

    loop(1, lines, send_third)
    own = paired(line)
    loop(1, lines, lambda z: third(z, z)[0].wait_recv())
    tops = st3r[:, 0, :]
    share = jnp.exp(tops - jnp.max(tops, axis=0, keepdims=True))
    share = share / jnp.sum(share * st3r[:, 1, :], axis=0, keepdims=True)
    spread(0, share)

    def add_third(i, attn):
        z = line_at(i)
        third(z, z)[1].wait_recv()
        return attn + o3r[z].astype(jnp.float32) * weight_s[z]

    attn = lax.fori_loop(1, lines, add_third, own * weight_s[line])
    flat = jnp.concatenate(
        [
            jnp.concatenate(
                [
                    attn[(r * heads + j) * steps : (r * heads + j + 1) * steps]
                    for r in range(reqs)
                ],
                0,
            )
            for j in range(heads)
        ],
        1,
    ).astype(jnp.bfloat16)
    weight_copy.wait()

    def term(which, z, half):
        at = pl.multiple_of(((2 * z + which) * 2 + half) * width, width)
        return jnp.dot(flat, w_s[:, pl.ds(at, width)], preferred_element_type=jnp.float32)

    def send_twin(which):
        def step(z):
            t1s[which * lines + z] = term(which, z, 1 - core)
            twin_term(which, z).start()

        loop(1, lines + 1, step)

    def twin_sum(which, z):
        mine = term(which, z, core)
        twin_term(which, z).wait_recv()
        return mine + t1r[which * lines + z]

    def send_mate(z):
        t2s[z] = twin_sum(other, z).astype(jnp.bfloat16)
        mate_term(z).start()

    def mate_sum(z):
        mine = twin_sum(side, z)
        mate_term(z).wait_recv()
        return mine + t2r[z].astype(jnp.float32)

    def send_line(z):
        t3s[z] = mate_sum(z).astype(jnp.bfloat16)
        line_term(z, line).start()

    send_twin(other)
    loop(1, lines + 1, send_mate)
    send_twin(side)
    loop(1, lines, send_line)
    own = mate_sum(line)

    def add_line(i, total):
        z = line_at(i)
        line_term(z, z).wait_recv()
        return total + t3r[z].astype(jnp.float32)

    out_ref[...] = lax.fori_loop(1, lines, add_line, own).astype(out_ref.dtype)

    def drain(z):
        for copy in (second(z), twin_term(0, z), twin_term(1, z), mate_term(z)):
            copy.wait_send()

    def drain_lines(z):
        for copy in third(z, line) + (line_term(z, line),):
            copy.wait_send()

    loop(1, lines + 1, drain)
    loop(1, lines, drain_lines)
    for copy in (stats_1, stats_2, first(0), first(1)):
        copy.wait_send()


def per_device(
    queries, new_keys, new_values, key_factors, key_basis, values, block_index, block_count,
    out_weight,
):
    devices = lax.axis_size("store")
    chips = devices // 2
    steps, reqs, n_heads, head_dim = queries.shape
    groups = new_keys.shape[2]
    group = n_heads // groups
    tokens = values.shape[1]
    rank = key_factors.shape[2]
    blocks = tokens // BLOCK
    heads_dev = n_heads // devices
    slots = block_index.shape[-1]
    half_group = group // 2
    part = half_group * steps
    wide = groups * head_dim
    chips_group = half_group // heads_dev

    cos_off, sin_off = rope_tables(np.arange(tokens), head_dim)
    base = np.stack(rope_tables(np.arange(devices) * tokens, head_dim), 1)
    sign = np.where(np.arange(head_dim) < head_dim // 2, -1.0, 1.0).astype(np.float32)
    cos_new, sin_new = rope_tables(tokens * devices + np.arange(steps), head_dim)
    head_order = np.arange(n_heads).reshape(groups, chips_group, 2, heads_dev)
    head_order = tuple(int(h) for h in head_order.swapaxes(1, 2).reshape(-1))
    lines = chips // 2
    place = [g if chips_group > 1 else (g % 2) * lines + g // 2 for g in range(groups)]
    lists = jnp.where(
        jnp.arange(slots, dtype=jnp.int32) < block_count[..., None], block_index, -1
    )
    expand = (np.arange(tokens)[None, :] // BLOCK == np.arange(blocks)[:, None]).astype(
        jnp.bfloat16
    )

    def whole(shape):
        return pl.BlockSpec(shape, lambda r: (0,) * len(shape))

    def per_request(shape):
        return pl.BlockSpec((1,) + shape, lambda r: (r,) + (0,) * len(shape))

    def of_request(shape):
        return pl.BlockSpec((steps, 1) + shape, lambda r: (0, r) + (0,) * len(shape))

    lanes = reqs * part
    out_block = pl.BlockSpec((groups, 1, part, head_dim), lambda r: (0, r, 0, 0))
    send, keep, stats = pl.pallas_call(
        functools.partial(attend_kernel, steps, head_dim, head_order, place),
        grid=(reqs,),
        out_shape=(
            jax.ShapeDtypeStruct((groups, reqs, part, head_dim), jnp.float32),
            jax.ShapeDtypeStruct((groups, reqs, part, head_dim), jnp.float32),
            jax.ShapeDtypeStruct((2, 2, groups, lanes), jnp.float32),
        ),
        in_specs=[
            whole((devices, 2, head_dim)),
            whole((tokens, head_dim)),
            whole((tokens, head_dim)),
            whole((steps, head_dim)),
            whole((steps, head_dim)),
            whole((blocks, tokens)),
            of_request((n_heads, head_dim)),
            of_request((groups, head_dim)),
            of_request((groups, head_dim)),
            of_request((groups, slots)),
            per_request((rank, tokens)),
            per_request((rank, wide)),
            per_request((tokens, wide)),
        ],
        out_specs=(out_block, out_block, whole((2, 2, groups, lanes))),
        scratch_shapes=[
            pltpu.VMEM((tokens, head_dim), jnp.float32),
            pltpu.VMEM((tokens, head_dim), jnp.float32),
            pltpu.VMEM((steps * (n_heads + groups), head_dim), jnp.float32),
            pltpu.VMEM((steps * groups, head_dim), jnp.float32),
            pltpu.VMEM((steps * groups * tokens // head_dim, head_dim), jnp.float32),
        ],
        compiler_params=pltpu.CompilerParams(vmem_limit_bytes=60 * 2**20),
        name="attend",
    )(
        base, cos_off, sin_off, cos_new, sin_new * sign, expand, queries, new_keys, new_values,
        lists, key_factors.swapaxes(1, 2), key_basis, values,
    )
    rows_dev = reqs * heads_dev * steps

    def by_chip(y):
        if chips_group > 1:
            y = y.reshape(groups, reqs, chips_group, heads_dev * steps, head_dim)
            y = y.transpose(0, 2, 1, 3, 4).reshape(lines, 2, rows_dev, head_dim).swapaxes(0, 1)
        return y.reshape(2, lines, rows_dev, head_dim)

    if chips_group > 1:
        stats = stats.reshape(2, 2, groups, reqs, chips_group, heads_dev * steps)
        stats = stats.transpose(0, 1, 2, 4, 3, 5).reshape(2, 2, lines, 2, rows_dev)
        stats = stats.swapaxes(2, 3).reshape(2, 2, chips, rows_dev)

    width = out_weight.shape[1] // devices
    out_rows = reqs * steps
    dma = pltpu.SemaphoreType.DMA
    vmem = pl.BlockSpec(memory_space=pltpu.VMEM)
    out = pl.pallas_call(
        functools.partial(combine_kernel, chips, reqs, steps),
        out_shape=jax.ShapeDtypeStruct((out_rows, width), jnp.bfloat16),
        in_specs=[vmem, vmem, vmem, pl.BlockSpec(memory_space=pl.ANY)],
        out_specs=vmem,
        scratch_shapes=[
            pltpu.VMEM(out_weight.shape, out_weight.dtype),
            pltpu.VMEM((2, lines, rows_dev, head_dim), jnp.float32),
            pltpu.VMEM((2, chips, rows_dev), jnp.float32),
            pltpu.VMEM((2 * chips, rows_dev, head_dim), jnp.float32),
            pltpu.VMEM((lines, rows_dev, head_dim), jnp.float32),
            pltpu.VMEM((lines, rows_dev, head_dim), jnp.bfloat16),
            pltpu.VMEM((lines, rows_dev, head_dim), jnp.bfloat16),
            pltpu.VMEM((2, lines, rows_dev), jnp.float32),
            pltpu.VMEM((2, lines, rows_dev), jnp.float32),
            pltpu.VMEM((lines, rows_dev, head_dim), jnp.bfloat16),
            pltpu.VMEM((lines, rows_dev, head_dim), jnp.bfloat16),
            pltpu.VMEM((lines, 8, rows_dev), jnp.float32),
            pltpu.VMEM((lines, 8, rows_dev), jnp.float32),
            pltpu.VMEM((chips, out_rows, width), jnp.float32),
            pltpu.VMEM((chips, out_rows, width), jnp.float32),
        ]
        + [pltpu.VMEM((lines, out_rows, width), jnp.bfloat16)] * 4
        + [dma((5,)), dma((4, chips)), dma((10, lines))],
        compiler_params=pltpu.CompilerParams(
            collective_id=0, has_side_effects=True, vmem_limit_bytes=57 * 2**20
        ),
        name="combine",
    )(by_chip(send), by_chip(keep), stats, out_weight)
    return out.reshape(reqs, steps, width).transpose(1, 0, 2)


def solution(mesh):
    placed = (
        P(None, "parts", None, None),
        P(None, "parts", None, None),
        P(None, "parts", None, None),
        P("parts", "store", None),
        P("parts", None, None),
        P("parts", "store", None),
        P(None, "parts", None, None),
        P(None, "parts", None),
        P("store", None),
    )
    return jax.shard_map(
        per_device, mesh=mesh, in_specs=placed, out_specs=P(None, "parts", "store"), check_vma=False
    )
```

time: 51.2 us -> 40.1 us (0.78)
  Pallas kernels: 43.6 us -> 36.8 us
  local copies, waits for them, and re-layouts: 5.26 us -> 1.39 us
    pallas_call x1, Pallas kernels: 30.1 us -> 25.7 us  [per_device(): pl.pallas_call(functools.partial(combine_kernel, chips, reqs, steps), out...]
    unnamed x3 -> x0, local copies, waits for them, and re-layouts: 3.12 us -> none
    pallas_call x1, Pallas kernels: 13.5 us -> 11.1 us  [per_device(): pl.pallas_call(functools.partial(attend_kernel, steps, head_dim, head_ord...]
    transpose x2 -> x0, other arithmetic: 1.94 us -> none  [the longest x1 1.01 us: per_device(): lists = lists.transpose(1, 2, 0, 3).reshape(reqs, groups * steps, slots)]
    select_n x0 -> x1, other arithmetic: none -> 1.66 us  [per_device(): jnp.where(jnp.arange(slots, dtype=jnp.int32) < block_count[..., None], bl...]
    transpose x1 -> x0, local copies, waits for them, and re-layouts: 0.75 us -> none  [per_device(): lists = lists.transpose(1, 2, 0, 3).reshape(reqs, groups * steps, slots)]
where the time goes in v2:
time: 40.1 us; the launch traced here: 39.9 us
  Pallas kernels  36.8 us (92%)
  other arithmetic  1.66 us (4%)
  local copies, waits for them, and re-layouts  1.39 us (3%)
    pallas_call x1, Pallas kernels, per_device(): pl.pallas_call(functools.partial(combine_kernel, chips, reqs, steps), out...  25.7 us
    pallas_call x1, Pallas kernels, per_device(): pl.pallas_call(functools.partial(attend_kernel, steps, head_dim, head_ord...  11.1 us
    select_n x1, other arithmetic, per_device(): jnp.where(jnp.arange(slots, dtype=jnp.int32) < block_count[..., None], bl...  1.66 us
    reshape x1, local copies, waits for them, and re-layouts, per_device(): return out.reshape(reqs, steps, width).transpose(1, 0, 2)  1.39 us

profile of v2, /device:TPU:0, one launch (start us, length us, event | category | flops | bytes accessed | tf_op | source)
XLA Modules:
  0.0 39.9 jit_solution(11695140788894620871)
XLA Ops:
  0.0 1.7 %fusion.list_ref = s32[8,4,8,64]{3,2,1,0:T(8,128)} fusion(s32[8,4,8,64]{3,2,1,0:T(8,128)} %param.21, s32[8,4,8]{2,1,0:T(4,128)} %param.22), kind=kLoop, calls=%fused_computation.1 | loop fusion | flops 32768 | bytes 132096 | tf_op jit(solution)/shard_map/jit(_where)/select_n | solution.py:428
  1.7 11.1 %attend.1 = (f32[8,4,32,128]{3,2,1,0:T(8,128)}, f32[8,4,32,128]{3,2,1,0:T(8,128)}, f32[2,2,8,128]{3,2,1,0:T(8,128)}) custom-call(f32[16,2,128]{2,1,0:T(2,128)} %constant.14.clone.base_ref, f32[512,128]{1,0:T(8,128)} %constant.15.clone.cos_ref, f32[512,128]{1,0:T(8,128)} %constant.16.clone.sin_ref, f32[8,128]{1,0:T(8,128)} %constant.17.clone.new_cos_ref, ...), custom_call_target="tpu_custom_call" | custom-call | tf_op jit(solution)/shard_map/attend/pallas_call | solution.py:446
  12.8 25.7 %combine.1 = bf16[32,512]{1,0:T(8,128)(2,1)} custom-call(f32[2,4,128,128]{3,2,1,0:T(8,128)} %bitcast.8, f32[2,4,128,128]{3,2,1,0:T(8,128)} %bitcast.9, f32[2,2,8,128]{3,2,1,0:T(8,128)} %get-tuple-element.10.st_ref, bf16[512,8192]{1,0:T(8,128)(2,1)} %w_ref.1), custom_call_target="tpu_custom_call" | custom-call | tf_op jit(solution)/shard_map/combine/pallas_call | solution.py:500
  38.5 1.4 %copy.18 = bf16[4,8,512]{2,0,1:T(4,128)(2,1)} copy(bf16[4,8,512]{2,1,0:T(8,128)(2,1)} %bitcast.10) | data formatting | bytes 65536 | tf_op jit(solution)/shard_map/reshape | solution.py:529

commit v3 on v2

--- a/solution.py
+++ b/solution.py
@@ -223,7 +223,7 @@
             step(line_at(i))
             return carry
 
-        lax.fori_loop(start, stop, body, 0)
+        lax.fori_loop(start, stop, body, 0, unroll=lines <= 4)
 
     stats_1 = remote(st_ref.at[1 - core], st1, sem.at[1], sem.at[2], twin)
     stats_2 = remote(st2s, st2r, sem.at[3], sem.at[4], mate)
@@ -326,7 +326,7 @@
         third(z, z)[1].wait_recv()
         return attn + o3r[z].astype(jnp.float32) * weight_s[z]
 
-    attn = lax.fori_loop(1, lines, add_third, own * weight_s[line])
+    attn = lax.fori_loop(1, lines, add_third, own * weight_s[line], unroll=lines <= 4)
     flat = jnp.concatenate(
         [
             jnp.concatenate(
@@ -382,7 +382,7 @@
         line_term(z, z).wait_recv()
         return total + t3r[z].astype(jnp.float32)
 
-    out_ref[...] = lax.fori_loop(1, lines, add_line, own).astype(out_ref.dtype)
+    out_ref[...] = lax.fori_loop(1, lines, add_line, own, unroll=lines <= 4).astype(out_ref.dtype)
 
     def drain(z):
         for copy in (second(z), twin_term(0, z), twin_term(1, z), mate_term(z)):

time: 40.1 us -> 40 us (level)
  no operation moved by 1% of the time
where the time goes in v3:
time: 40 us; the launch traced here: 39.8 us
  Pallas kernels  36.8 us (92%)
  other arithmetic  1.66 us (4%)
  local copies, waits for them, and re-layouts  1.39 us (3%)
    pallas_call x1, Pallas kernels, per_device(): pl.pallas_call(functools.partial(combine_kernel, chips, reqs, steps), out...  25.6 us
    pallas_call x1, Pallas kernels, per_device(): pl.pallas_call(functools.partial(attend_kernel, steps, head_dim, head_ord...  11.1 us
    select_n x1, other arithmetic, per_device(): jnp.where(jnp.arange(slots, dtype=jnp.int32) < block_count[..., None], bl...  1.66 us
    reshape x1, local copies, waits for them, and re-layouts, per_device(): return out.reshape(reqs, steps, width).transpose(1, 0, 2)  1.39 us

profile of v3, /device:TPU:0, one launch (start us, length us, event | category | flops | bytes accessed | tf_op | source)
XLA Modules:
  0.0 39.8 jit_solution(16112008335808626355)
XLA Ops:
  0.0 1.7 %fusion.list_ref = s32[8,4,8,64]{3,2,1,0:T(8,128)} fusion(s32[8,4,8,64]{3,2,1,0:T(8,128)} %param.21, s32[8,4,8]{2,1,0:T(4,128)} %param.22), kind=kLoop, calls=%fused_computation.1 | loop fusion | flops 32768 | bytes 132096 | tf_op jit(solution)/shard_map/jit(_where)/select_n | solution.py:428
  1.7 11.1 %attend.1 = (f32[8,4,32,128]{3,2,1,0:T(8,128)}, f32[8,4,32,128]{3,2,1,0:T(8,128)}, f32[2,2,8,128]{3,2,1,0:T(8,128)}) custom-call(f32[16,2,128]{2,1,0:T(2,128)} %constant.14.clone.base_ref, f32[512,128]{1,0:T(8,128)} %constant.15.clone.cos_ref, f32[512,128]{1,0:T(8,128)} %constant.16.clone.sin_ref, f32[8,128]{1,0:T(8,128)} %constant.17.clone.new_cos_ref, ...), custom_call_target="tpu_custom_call" | custom-call | tf_op jit(solution)/shard_map/attend/pallas_call | solution.py:446
  12.8 25.6 %combine.1 = bf16[32,512]{1,0:T(8,128)(2,1)} custom-call(f32[2,4,128,128]{3,2,1,0:T(8,128)} %bitcast.8, f32[2,4,128,128]{3,2,1,0:T(8,128)} %bitcast.9, f32[2,2,8,128]{3,2,1,0:T(8,128)} %get-tuple-element.10.st_ref, bf16[512,8192]{1,0:T(8,128)(2,1)} %w_ref.1), custom_call_target="tpu_custom_call" | custom-call | tf_op jit(solution)/shard_map/combine/pallas_call | solution.py:500
  38.4 1.4 %copy.18 = bf16[4,8,512]{2,0,1:T(4,128)(2,1)} copy(bf16[4,8,512]{2,1,0:T(8,128)(2,1)} %bitcast.10) | data formatting | bytes 65536 | tf_op jit(solution)/shard_map/reshape | solution.py:529

commit v4 on v3

--- a/solution.py
+++ b/solution.py
@@ -36,7 +36,7 @@
 
 def attend_kernel(
     steps, head_dim, head_order, place, base_ref, cos_ref, sin_ref, new_cos_ref, new_sin_ref,
-    expand_ref, q_ref, nk_ref, nv_ref, list_ref, factor_ref, basis_ref, value_ref, send_ref,
+    expand_ref, q_ref, nk_ref, nv_ref, list_ref, count_ref, factor_ref, basis_ref, value_ref, send_ref,
     keep_ref, stat_ref, cos_s, sin_s, head_s, nv_s, bias_s,
 ):
     r = pl.program_id(0)
@@ -69,6 +69,8 @@
         stat_ref[...] = jnp.zeros_like(stat_ref)
 
     listed = list_ref[:, 0].reshape(steps * groups, slots).astype(jnp.float32).T
+    slot_ids = lax.broadcasted_iota(jnp.int32, (slots, steps * groups), 0)
+    listed = jnp.where(slot_ids < count_ref[0], listed, -1.0)
     block_ids = (
         lax.broadcasted_iota(jnp.int32, (blocks, groups * steps), 0) + me * blocks
     ).astype(jnp.float32)
@@ -425,9 +427,7 @@
     head_order = tuple(int(h) for h in head_order.swapaxes(1, 2).reshape(-1))
     lines = chips // 2
     place = [g if chips_group > 1 else (g % 2) * lines + g // 2 for g in range(groups)]
-    lists = jnp.where(
-        jnp.arange(slots, dtype=jnp.int32) < block_count[..., None], block_index, -1
-    )
+    counts = block_count.transpose(1, 0, 2).reshape(reqs, 1, steps * groups)
     expand = (np.arange(tokens)[None, :] // BLOCK == np.arange(blocks)[:, None]).astype(
         jnp.bfloat16
     )
@@ -462,6 +462,7 @@
             of_request((groups, head_dim)),
             of_request((groups, head_dim)),
             of_request((groups, slots)),
+            per_request((1, steps * groups)),
             per_request((rank, tokens)),
             per_request((rank, wide)),
             per_request((tokens, wide)),
@@ -478,7 +479,7 @@
         name="attend",
     )(
         base, cos_off, sin_off, cos_new, sin_new * sign, expand, queries, new_keys, new_values,
-        lists, key_factors.swapaxes(1, 2), key_basis, values,
+        block_index, counts, key_factors.swapaxes(1, 2), key_basis, values,
     )
     rows_dev = reqs * heads_dev * steps
 

time: 40 us -> 39.9 us (level)
  other arithmetic: 1.66 us -> 0 us
  local copies, waits for them, and re-layouts: 1.39 us -> 2.78 us
    select_n x1 -> x0, other arithmetic: 1.66 us -> none  [per_device(): jnp.where(jnp.arange(slots, dtype=jnp.int32) < block_count[..., None], bl...]
    transpose x0 -> x1, local copies, waits for them, and re-layouts: none -> 0.72 us  [per_device(): counts = block_count.transpose(1, 0, 2).reshape(reqs, 1, steps * groups)]
    reshape x0 -> x1, local copies, waits for them, and re-layouts: none -> 0.67 us  [per_device(): counts = block_count.transpose(1, 0, 2).reshape(reqs, 1, steps * groups)]
where the time goes in v4:
time: 39.9 us; the launch traced here: 39.6 us
  Pallas kernels  36.8 us (92%)
  local copies, waits for them, and re-layouts  2.78 us (7%)
    pallas_call x1, Pallas kernels, per_device(): pl.pallas_call(functools.partial(combine_kernel, chips, reqs, steps), out...  25.6 us
    pallas_call x1, Pallas kernels, per_device(): pl.pallas_call(functools.partial(attend_kernel, steps, head_dim, head_ord...  11.2 us
    reshape x1, local copies, waits for them, and re-layouts, per_device(): return out.reshape(reqs, steps, width).transpose(1, 0, 2)  1.39 us

profile of v4, /device:TPU:0, one launch (start us, length us, event | category | flops | bytes accessed | tf_op | source)
XLA Modules:
  0.0 39.6 jit_solution(11197368945586320431)
XLA Ops:
  0.0 0.7 %copy.16 = s32[4,8,8]{2,1,0:T(8,128)S(1)} copy(s32[4,8,8]{2,0,1:T(4,128)} %bitcast.12) | data formatting | bytes 2048 | tf_op jit(solution)/shard_map/transpose | solution.py:430
  0.7 0.7 %reshape.12.count_ref = s32[4,1,64]{2,1,0:T(1,128)} reshape(s32[4,8,8]{2,1,0:T(8,128)S(1)} %copy.16) | data formatting | bytes 2048 | tf_op jit(solution)/shard_map/reshape | solution.py:430
  1.4 11.2 %attend.1 = (f32[8,4,32,128]{3,2,1,0:T(8,128)}, f32[8,4,32,128]{3,2,1,0:T(8,128)}, f32[2,2,8,128]{3,2,1,0:T(8,128)}) custom-call(f32[16,2,128]{2,1,0:T(2,128)} %constant.12.clone.base_ref, f32[512,128]{1,0:T(8,128)} %constant.13.clone.cos_ref, f32[512,128]{1,0:T(8,128)} %constant.14.clone.sin_ref, f32[8,128]{1,0:T(8,128)} %constant.15.clone.new_cos_ref, ...), custom_call_target="tpu_custom_call" | custom-call | tf_op jit(solution)/shard_map/attend/pallas_call | solution.py:446
  12.6 25.6 %combine.1 = bf16[32,512]{1,0:T(8,128)(2,1)} custom-call(f32[2,4,128,128]{3,2,1,0:T(8,128)} %bitcast.9, f32[2,4,128,128]{3,2,1,0:T(8,128)} %bitcast.10, f32[2,2,8,128]{3,2,1,0:T(8,128)} %get-tuple-element.10.st_ref, bf16[512,8192]{1,0:T(8,128)(2,1)} %w_ref.1), custom_call_target="tpu_custom_call" | custom-call | tf_op jit(solution)/shard_map/combine/pallas_call | solution.py:501
  38.2 1.4 %copy.19 = bf16[4,8,512]{2,0,1:T(4,128)(2,1)} copy(bf16[4,8,512]{2,1,0:T(8,128)(2,1)} %bitcast.11) | data formatting | bytes 65536 | tf_op jit(solution)/shard_map/reshape | solution.py:530
